TPU v7x, 32 devices: a whole 2x2x4 slice. The times are simulated.
32 devices in a mesh: grp: 2 (over x), site: 16 (over z, y, core).
Axes of the slice: x: 2, y: 2, z: 4, core: 2. Of those that a mesh axis runs over, the one named last changes fastest.
Arguments:
- psi: bfloat16 [128, 128, 128], P(('grp', 'site')), parts along dimension 0, may hold values from -6 to 6
- left_env: bfloat16 [128, 34, 128, 128], P(('grp', 'site')), parts along dimension 0, may hold values from -1 to 2
- right_env: bfloat16 [128, 34, 128, 128], P(('grp', 'site')), parts along dimension 0, may hold values from -2 to 2
- mpo_shift: int32 [34], replicated, may hold values from -1 to 1
- block_sizes: int32 [128, 2], P(('grp', 'site')), parts along dimension 0, may hold values from 64 to 128
Outputs:
- krylov: bfloat16 [128, 128, 128], P(('grp', 'site')), parts along dimension 0
- image: bfloat16 [128, 128, 128], P(('grp', 'site')), parts along dimension 0
- coefficients: float32 [10], P('grp'), parts along dimension 0
There are 2 independent parts, one for each index of `grp`. A program takes and returns all parts, laid end to end along the dimension named above; an argument that names none is the same for every part. Nothing has to cross between parts.
Inputs may be any that keep to these rules, and one draw needn't show every extreme that they name: `mpo_shift`: each MPO index moves the sector by -1, 0 or +1.
All inputs are finite; a program needn't handle non-finite values.
Results may differ from a plain program's by a relative error of at most 0.013.
Values may be sent and summed in bfloat16 or wider, within the bound.
A program may use at most 64 MiB of HBM per device.

v0:
```python
import functools

import jax
import jax.numpy as jnp
from jax import lax
from jax.experimental import pallas as pl
from jax.experimental.pallas import tpu as pltpu
from jax.sharding import PartitionSpec as P

F32 = jnp.float32
BF16 = jnp.bfloat16
EPS = 1e-06
PIECE = 6


def kernel(
    n, cap, shift_ref, sizes_ref, psi_ref, left_hbm, right_hbm,
    kry_ref, img_ref, coef_ref,
    lbuf, rbuf, edge, halo, pack, prod, where_at, nexts, u_ref, ue_ref, v_ref, ve_ref, live_ref,
    h_ref, t_ref, te_ref, part_ref, red_ref,
    load_sem, edge_sem, usend, urecv, hsend, hrecv, tsend, trecv, rsend, rrecv,
):
    sectors, width = psi_ref.shape[0], psi_ref.shape[1]
    count = shift_ref.shape[0]
    last = sectors - 1
    cells = float(n * sectors * width * width)
    me = lax.axis_index("site")
    has_left, has_right = me > 0, me < n - 1

    edges = []
    for side, sector in enumerate((last, 0)):
        copy = pltpu.make_async_copy(right_hbm.at[sector], edge.at[pl.ds(side * count, count)], edge_sem.at[side])
        copy.start()
        edges.append(copy)
    loads = []
    for i, (src, dst) in enumerate(((right_hbm, rbuf), (left_hbm, lbuf))):
        for a in range(sectors):
            copy = pltpu.make_async_copy(src.at[a], dst.at[pl.ds(a * count, count)], load_sem.at[i * sectors + a])
            copy.start()
            loads.append(copy)

    barrier = pltpu.get_barrier_semaphore()

    def greet(k, _):
        pl.semaphore_signal(
            barrier, inc=1, device_id={"site": lax.rem(me + k, n)}, device_id_type=pl.DeviceIdType.MESH
        )
        return 0

    lax.fori_loop(1, n, greet, 0)

    nl = jnp.int32(count)
    nr = jnp.int32(count)
    nexts[0, count] = nl
    nexts[1, count] = nr
    for w in range(count - 1, -1, -1):
        s = shift_ref[w]
        nexts[0, w] = nl
        nexts[1, w] = nr
        nl = jnp.where(s == -1, w, nl)
        nr = jnp.where(s == 1, w, nr)
    def remote(src, dst, ssem, rsem, to):
        return pltpu.make_async_remote_copy(
            src_ref=src, dst_ref=dst, send_sem=ssem, recv_sem=rsem,
            device_id={"site": to}, device_id_type=pl.DeviceIdType.MESH,
        )

    def swap(first_src, last_src, dst, ssem, rsem):
        right = remote(last_src, dst.at[0], ssem.at[0], rsem.at[0], jnp.minimum(me + 1, n - 1))
        left = remote(first_src, dst.at[1], ssem.at[1], rsem.at[1], jnp.maximum(me - 1, 0))
        return right, left

    def start(pair):
        pl.when(has_right)(lambda: pair[0].start())
        pl.when(has_left)(lambda: pair[1].start())

    def finish(pair):
        @pl.when(has_left)
        def _():
            pair[0].wait_recv()
            pair[1].wait_send()

        @pl.when(has_right)
        def _():
            pair[1].wait_recv()
            pair[0].wait_send()

    rows = lax.broadcasted_iota(jnp.int32, (width, width), 0)
    cols = lax.broadcasted_iota(jnp.int32, (width, width), 1)
    for a in range(sectors):
        keep = (rows < sizes_ref[0:1, a : a + 1]) & (cols < sizes_ref[1:2, a : a + 1])
        mask = jnp.where(keep, 1.0, 0.0).astype(F32)
        live_ref[a] = mask
        u_ref[a] = (psi_ref[a].astype(F32) * mask).astype(BF16)

    for copy in edges:
        copy.wait()

    def packing(j, at):
        at_low, at_high = at
        pack[0, j] = edge[jnp.minimum(at_low, count - 1)]
        pack[1, j] = edge[count + jnp.minimum(at_high, count - 1)]
        return nexts[0, at_low], nexts[1, at_high]

    at = (nl, nr)
    pieces = []
    for i, begin in enumerate(range(0, cap, PIECE)):
        size = min(PIECE, cap - begin)
        at = lax.fori_loop(begin, begin + size, packing, at)
        if i == 0:
            pl.semaphore_wait(barrier, n - 1)
            u_pair = swap(u_ref.at[0], u_ref.at[last], ue_ref, usend, urecv)
            start(u_pair)
        some = pl.ds(begin, size)
        right = remote(
            pack.at[0, some], halo.at[0, some], hsend.at[0, i], hrecv.at[0, i], jnp.minimum(me + 1, n - 1)
        )
        left = remote(
            pack.at[1, some], halo.at[1, some], hsend.at[1, i], hrecv.at[1, i], jnp.maximum(me - 1, 0)
        )
        start((right, left))
        pieces.append((begin, size, (right, left)))

    low = jnp.int32(sectors * count)
    high = jnp.int32(sectors * count + cap)
    for w in range(count):
        s = shift_ref[w]
        for a in range(sectors):
            place = (a + s) * count + w
            if a == 0:
                place = jnp.where(s == -1, low, place)
            if a == last:
                place = jnp.where(s == 1, high, place)
            where_at[a, w] = place
        low = low + jnp.where(s == -1, 1, 0)
        high = high + jnp.where(s == 1, 1, 0)

    @pl.when(me == 0)
    def _():
        ue_ref[0] = jnp.zeros((width, width), BF16)
        te_ref[0, 0] = jnp.zeros((width, width), F32)
        te_ref[1, 0] = jnp.zeros((width, width), F32)
        halo[0] = jnp.zeros((cap, width, width), BF16)

    @pl.when(me == n - 1)
    def _():
        ue_ref[1] = jnp.zeros((width, width), BF16)
        te_ref[0, 1] = jnp.zeros((width, width), F32)
        te_ref[1, 1] = jnp.zeros((width, width), F32)
        halo[1] = jnp.zeros((cap, width, width), BF16)


    group = 2 if count % 2 == 0 and cap % 2 == 0 else 1

    def products(vector, envir, base, first):
        rhs = [envir[base + first + i] for i in range(group)]
        rhs = rhs[0] if group == 1 else jnp.concatenate(rhs, axis=1)
        return jnp.dot(vector, rhs, preferred_element_type=F32).astype(BF16)

    def local_products(vec):
        def body(p, _):
            for b in range(sectors):
                out = products(vec[b], rbuf, b * count, p * group)
                for i in range(group):
                    prod[b * count + p * group + i] = out[:, i * width : (i + 1) * width]
            return 0

        lax.fori_loop(0, count // group, body, 0)

    def halo_products(vec, begin=0, size=cap):
        def body(p, _):
            for side in range(2):
                out = products(vec[side], halo.at[side], 0, p * group)
                for i in range(group):
                    prod[sectors * count + side * cap + p * group + i] = out[:, i * width : (i + 1) * width]
            return 0

        lax.fori_loop(begin // group, (begin + size) // group, body, 0)

    chunk = count // 2 if count % 2 == 0 else count

    def left_side(places, c, _):
        for a in places:
            lhs = jnp.concatenate([lbuf[a * count + c * chunk + i] for i in range(chunk)], axis=1)
            rhs = jnp.concatenate([prod[where_at[a, c * chunk + i]] for i in range(chunk)], axis=0)
            out = jnp.dot(lhs, rhs, preferred_element_type=F32)
            h_ref[a] = h_ref[a] + out * live_ref[a]
        return 0

    def apply_left(places):
        for a in places:
            h_ref[a] = jnp.zeros((width, width), F32)
        lax.fori_loop(0, count // chunk, functools.partial(left_side, places), 0)

    def flat(x):
        return x.reshape(sectors * width, width)

    def summed(x):
        return jnp.sum(jnp.sum(x, axis=0, keepdims=True), axis=1, keepdims=True)

    def reduce_start(step, sums):
        at = lax.broadcasted_iota(jnp.int32, (1, width), 1)
        row = jnp.zeros((1, width), F32)
        for q, value in enumerate(sums):
            row = jnp.where(at == q, value, row)
        part_ref[step] = row
        red_ref[step, me] = row

        def send(k, _):
            remote(
                part_ref.at[step], red_ref.at[step, me], rsend.at[step, k], rrecv.at[step, me],
                lax.rem(me + k, n),
            ).start()
            return 0

        lax.fori_loop(1, n, send, 0)

    def reduce_finish(step):
        def wait(k, _):
            j = lax.rem(me + k, n)
            got = remote(part_ref.at[step], red_ref.at[step, j], rsend.at[step, k], rrecv.at[step, j], j)
            got.wait_recv()
            got.wait_send()
            return 0

        lax.fori_loop(1, n, wait, 0)
        got = red_ref[step].reshape(n, width)
        return [got[:, q : q + 1] for q in range(4)]

    def total(x):
        return jnp.sum(x, axis=0, keepdims=True) / cells

    def ratio(top, bottom):
        return jnp.where(bottom > 0.0, top / jnp.where(bottom > 0.0, bottom, 1.0), 0.0)

    for copy in loads[:sectors]:
        copy.wait()
    local_products(u_ref)
    for copy in loads[sectors:]:
        copy.wait()
    inner, outer = tuple(range(1, last)), tuple(sorted({0, last}))
    if inner:
        apply_left(inner)
    finish(u_pair)
    for begin, size, pair in pieces:
        finish(pair)
        halo_products(ue_ref, begin, size)
    apply_left(outer)
    u = flat(u_ref[...]).astype(F32)
    g = flat(h_ref[...])
    uu, ug = summed(u * u), summed(u * g)
    r = g - ratio(ug, uu) * u
    reduce_start(0, [uu, ug, summed(r * r)])
    t_pair = swap(h_ref.at[0], h_ref.at[last], te_ref.at[0], tsend.at[0], trecv.at[0])
    start(t_pair)
    uu, ug, rr, _ = reduce_finish(0)
    scale2 = total(uu) + EPS
    inv_scale = lax.rsqrt(scale2)
    alpha1 = total(ug) / scale2
    off = ratio(ug, uu) - alpha1
    beta1 = jnp.sqrt(total(rr + off * off * uu) / scale2 + EPS)
    down = inv_scale / beta1
    for a in range(sectors):
        v_ref[a] = ((h_ref[a] - alpha1 * u_ref[a].astype(F32)) * down).astype(BF16)

    local_products(v_ref)
    if inner:
        apply_left(inner)
    finish(t_pair)
    for side in range(2):
        ve_ref[side] = ((te_ref[0, side] - alpha1 * ue_ref[side].astype(F32)) * down).astype(BF16)
    halo_products(ve_ref)
    apply_left(outer)
    v = flat(v_ref[...]).astype(F32)
    h = flat(h_ref[...])
    t = h - (beta1 * inv_scale) * flat(u_ref[...]).astype(F32)
    t_ref[...] = t.reshape(t_ref.shape)
    vv, vh, vt = summed(v * v), summed(v * h), summed(v * t)
    r = t - ratio(vt, vv) * v
    reduce_start(1, [vv, vh, vt, summed(r * r)])
    t_pair = swap(t_ref.at[0], t_ref.at[last], te_ref.at[1], tsend.at[1], trecv.at[1])
    start(t_pair)
    vv, vh, vt, rr = reduce_finish(1)
    alpha2 = total(vh)
    off = ratio(vt, vv) - alpha2
    beta2 = jnp.sqrt(total(rr + off * off * vv) + EPS)
    down = 1.0 / beta2
    for a in range(sectors):
        kry_ref[a] = ((t_ref[a] - alpha2 * v_ref[a].astype(F32)) * down).astype(BF16)

    local_products(kry_ref)
    if inner:
        apply_left(inner)
    finish(t_pair)
    for side in range(2):
        ve_ref[side] = ((te_ref[1, side] - alpha2 * ve_ref[side].astype(F32)) * down).astype(BF16)
    halo_products(ve_ref)
    apply_left(outer)
    reduce_start(2, [summed(flat(kry_ref[...]).astype(F32) * flat(h_ref[...]))])
    img_ref[...] = h_ref[...].astype(BF16)
    alpha3 = total(reduce_finish(2)[0])
    lane = lax.broadcasted_iota(jnp.int32, coef_ref.shape, 1)
    out = jnp.zeros(coef_ref.shape, F32)
    for i, value in enumerate((alpha1, alpha2, alpha3, beta1, beta2)):
        out = jnp.where(lane == i, value, out)
    coef_ref[...] = out


def call(n, cap, collective, psi, left_env, right_env, mpo_shift, block_sizes):
    sectors, width = psi.shape[0], psi.shape[1]
    count = mpo_shift.shape[0]
    vmem = pl.BlockSpec(memory_space=pltpu.VMEM)
    smem = pl.BlockSpec(memory_space=pltpu.SMEM)
    hbm = pl.BlockSpec(memory_space=pl.ANY)
    block = (width, width)
    dma = pltpu.SemaphoreType.DMA
    pieces = -(-cap // PIECE)
    return pl.pallas_call(
        functools.partial(kernel, n, cap),
        out_shape=(
            jax.ShapeDtypeStruct(psi.shape, BF16),
            jax.ShapeDtypeStruct(psi.shape, BF16),
            jax.ShapeDtypeStruct((1, width), F32),
        ),
        in_specs=[smem, vmem, vmem, hbm, hbm],
        out_specs=(vmem, vmem, vmem),
        scratch_shapes=[
            pltpu.VMEM((sectors * count,) + block, BF16),
            pltpu.VMEM((sectors * count,) + block, BF16),
            pltpu.VMEM((2 * count,) + block, BF16),
            pltpu.VMEM((2, cap) + block, BF16),
            pltpu.VMEM((2, cap) + block, BF16),
            pltpu.VMEM((sectors * count + 2 * cap,) + block, BF16),
            pltpu.SMEM((sectors, count), jnp.int32),
            pltpu.SMEM((2, count + 1), jnp.int32),
            pltpu.VMEM((sectors,) + block, BF16),
            pltpu.VMEM((2,) + block, BF16),
            pltpu.VMEM((sectors,) + block, BF16),
            pltpu.VMEM((2,) + block, BF16),
            pltpu.VMEM((sectors,) + block, F32),
            pltpu.VMEM((sectors,) + block, F32),
            pltpu.VMEM((sectors,) + block, F32),
            pltpu.VMEM((2, 2) + block, F32),
            pltpu.VMEM((3, 1, width), F32),
            pltpu.VMEM((3, n, 1, width), F32),
            dma((2 * sectors,)),
            dma((2,)), dma((2,)), dma((2,)),
            dma((2, pieces)), dma((2, pieces)),
            dma((2, 2)), dma((2, 2)),
            dma((3, n)), dma((3, n)),
        ],
        compiler_params=pltpu.CompilerParams(
            collective_id=collective, has_side_effects=True, vmem_limit_bytes=56 * 1024 * 1024
        ),
    )(mpo_shift, block_sizes, psi, left_env, right_env)


def write_out(kry_in, img_in, coef_in, kry_ref, img_ref, coef_ref):
    kry_ref[...] = kry_in[...]
    img_ref[...] = img_in[...]
    for i in range(coef_ref.shape[0]):
        coef_ref[i] = coef_in[0, i]


def shards(n, psi, left_env, right_env, mpo_shift, block_sizes):
    count = mpo_shift.shape[0]
    args = (psi, left_env, right_env, mpo_shift, block_sizes.T)
    caps = sorted({min(14, count), min(18, count), count})
    most = jnp.maximum(jnp.sum(mpo_shift == -1), jnp.sum(mpo_shift == 1))
    which = sum((most > cap).astype(jnp.int32) for cap in caps[:-1])
    branches = [functools.partial(call, n, cap, i) for i, cap in enumerate(caps)]
    krylov, image, coefficients = lax.switch(which, branches, *args)
    vmem = pl.BlockSpec(memory_space=pltpu.VMEM)
    return pl.pallas_call(
        write_out,
        out_shape=(
            jax.ShapeDtypeStruct(psi.shape, BF16),
            jax.ShapeDtypeStruct(psi.shape, BF16),
            jax.ShapeDtypeStruct((5,), F32),
        ),
        in_specs=[vmem] * 3,
        out_specs=(vmem, vmem, pl.BlockSpec(memory_space=pltpu.SMEM)),
    )(krylov, image, coefficients)


def solution(mesh):
    in_specs = (
        P(("grp", "site"), None, None),
        P(("grp", "site"), None, None, None),
        P(("grp", "site"), None, None, None),
        P(),
        P(("grp", "site"), None),
    )
    out_specs = (P(("grp", "site"), None, None), P(("grp", "site"), None, None), P("grp"))
    return jax.shard_map(
        functools.partial(shards, mesh.shape["site"]),
        mesh=mesh, in_specs=in_specs, out_specs=out_specs, check_vma=False,
    )
```

profile of v0, /device:TPU:0, one launch (start us, length us, event | category | flops | bytes accessed | tf_op | source)
XLA Modules:
  0.0 54.2 jit_solution(14166714595771985900)
XLA Ops:
  0.6 1.3 %fusion.1 = (s32[]{:T(128)}, s32[]{:T(128)}) fusion(s32[34]{0:T(128)} %param.11), kind=kLoop, calls=%fused_computation.3 | loop fusion | flops 202 | bytes 144 | tf_op jit(solution)/shard_map/reduce_sum | solution.py:369
  3.2 50.0 %conditional.1 = ((bf16[4,128,128]{2,1,0:T(8,128)(2,1)S(1)}, bf16[4,128,128]{2,1,0:T(8,128)(2,1)S(1)}, f32[1,128]{1,0:T(1,128)S(1)})) conditional(s32[]{:T(128)} %clamp.3, (s32[34]{0:T(128)}, s32[2,4]{1,0:T(2,128)}, bf16[4,128,128]{2,1,0:T(8,128)(2,1)}, bf16[4,34,128,128]{3,2,1,0:T(8,128)(2,1)}, ...), branch_computations={%region_2.0_spmd, %region_3.0_spmd, %region_4.0_spmd} | conditional | bytes 8 | solution.py:372
  3.2 49.8 %branch_0_fun.1 = (bf16[4,128,128]{2,1,0:T(8,128)(2,1)S(1)}, bf16[4,128,128]{2,1,0:T(8,128)(2,1)S(1)}, f32[1,128]{1,0:T(1,128)S(1)}) custom-call(s32[34]{0:T(128)} %get-tuple-element.30.shift_ref, s32[2,4]{1,0:T(2,128)} %get-tuple-element.31.sizes_ref, bf16[4,128,128]{2,1,0:T(8,128)(2,1)} %get-tuple-element.32.psi_ref, ...), custom_call_target="tpu_custom_call" | custom-call | tf_op jit(solution)/shard_map/cond/branch_0_fun/pallas_call | solution.py:318
  53.3 0.7 %shard_map.76 = (bf16[4,128,128]{2,1,0:T(8,128)(2,1)}, bf16[4,128,128]{2,1,0:T(8,128)(2,1)}, f32[5]{0:T(128)}) custom-call(bf16[4,128,128]{2,1,0:T(8,128)(2,1)S(1)} %get-tuple-element.51.kry_in, bf16[4,128,128]{2,1,0:T(8,128)(2,1)S(1)} %get-tuple-element.52.img_in, f32[1,128]{1,0:T(1,128)S(1)} %get-tuple-element.53.coef_in), custom_call_target="tpu_custom_call" | custom-call | tf_op jit(solution)/shard_map/pallas_call | solution.py:374
where the time goes:
time: 54.4 us; the launch traced here: 54.2 us
  Pallas kernels  50.5 us (93%)
  between operations  2.13 us (4%)
  other arithmetic  1.3 us (2%)
    pallas_call x1, Pallas kernels, call(): pl.pallas_call(functools.partial(kernel, n, cap), out_shape=(jax.ShapeDty...  49.8 us
    reduce_sum x1, other arithmetic, shards(): most = jnp.maximum(jnp.sum(mpo_shift == -1), jnp.sum(mpo_shift == 1))  1.3 us

commit v1 on v0

--- a/solution.py
+++ b/solution.py
@@ -26,6 +26,8 @@
     cells = float(n * sectors * width * width)
     me = lax.axis_index("site")
     has_left, has_right = me > 0, me < n - 1
+    plane = max(p for p in range(1, n + 1) if n % p == 0 and p * p <= n)
+    base = me // plane * plane
 
     edges = []
     for side, sector in enumerate((last, 0)):
@@ -207,23 +209,44 @@
         red_ref[step, me] = row
 
         def send(k, _):
+            to = base + lax.rem(me - base + k, plane)
             remote(
-                part_ref.at[step], red_ref.at[step, me], rsend.at[step, k], rrecv.at[step, me],
-                lax.rem(me + k, n),
+                part_ref.at[step], red_ref.at[step, me], rsend.at[step, k], rrecv.at[step, me], to
             ).start()
             return 0
 
-        lax.fori_loop(1, n, send, 0)
+        lax.fori_loop(1, plane, send, 0)
 
     def reduce_finish(step):
-        def wait(k, _):
-            j = lax.rem(me + k, n)
+        def near(k, _):
+            j = base + lax.rem(me - base + k, plane)
             got = remote(part_ref.at[step], red_ref.at[step, j], rsend.at[step, k], rrecv.at[step, j], j)
             got.wait_recv()
             got.wait_send()
             return 0
 
-        lax.fori_loop(1, n, wait, 0)
+        lax.fori_loop(1, plane, near, 0)
+
+        def rows_of(j):
+            return red_ref.at[step, pl.ds(j // plane * plane, plane)]
+
+        def pass_on(m, _):
+            to = lax.rem(me + m * plane, n)
+            remote(
+                rows_of(me), rows_of(me), rsend.at[step, plane - 1 + m], rrecv.at[step, me], to
+            ).start()
+            return 0
+
+        lax.fori_loop(1, n // plane, pass_on, 0)
+
+        def far(m, _):
+            j = lax.rem(me + m * plane, n)
+            got = remote(rows_of(j), rows_of(j), rsend.at[step, plane - 1 + m], rrecv.at[step, j], j)
+            got.wait_recv()
+            got.wait_send()
+            return 0
+
+        lax.fori_loop(1, n // plane, far, 0)
         got = red_ref[step].reshape(n, width)
         return [got[:, q : q + 1] for q in range(4)]
 

time: 54.4 us -> 60.4 us (1.11)
  Pallas kernels: 50.5 us -> 56.5 us
    pallas_call x1, Pallas kernels: 49.8 us -> 55.8 us  [call(): pl.pallas_call(functools.partial(kernel, n, cap), out_shape=(jax.ShapeDty...]
where the time goes in v1:
time: 60.4 us; the launch traced here: 60.2 us
  Pallas kernels  56.5 us (94%)
  between operations  2.13 us (4%)
  other arithmetic  1.3 us (2%)
    pallas_call x1, Pallas kernels, call(): pl.pallas_call(functools.partial(kernel, n, cap), out_shape=(jax.ShapeDty...  55.8 us
    reduce_sum x1, other arithmetic, shards(): most = jnp.maximum(jnp.sum(mpo_shift == -1), jnp.sum(mpo_shift == 1))  1.3 us

profile of v1, /device:TPU:0, one launch (start us, length us, event | category | flops | bytes accessed | tf_op | source)
XLA Modules:
  0.0 60.2 jit_solution(16444084241440628)
XLA Ops:
  0.6 1.3 %fusion.1 = (s32[]{:T(128)}, s32[]{:T(128)}) fusion(s32[34]{0:T(128)} %param.11), kind=kLoop, calls=%fused_computation.3 | loop fusion | flops 202 | bytes 144 | tf_op jit(solution)/shard_map/reduce_sum | solution.py:392
  3.2 56.0 %conditional.1 = ((bf16[4,128,128]{2,1,0:T(8,128)(2,1)S(1)}, bf16[4,128,128]{2,1,0:T(8,128)(2,1)S(1)}, f32[1,128]{1,0:T(1,128)S(1)})) conditional(s32[]{:T(128)} %clamp.3, (s32[34]{0:T(128)}, s32[2,4]{1,0:T(2,128)}, bf16[4,128,128]{2,1,0:T(8,128)(2,1)}, bf16[4,34,128,128]{3,2,1,0:T(8,128)(2,1)}, ...), branch_computations={%region_2.0_spmd, %region_3.0_spmd, %region_4.0_spmd} | conditional | bytes 8 | solution.py:395
  3.2 55.8 %branch_0_fun.1 = (bf16[4,128,128]{2,1,0:T(8,128)(2,1)S(1)}, bf16[4,128,128]{2,1,0:T(8,128)(2,1)S(1)}, f32[1,128]{1,0:T(1,128)S(1)}) custom-call(s32[34]{0:T(128)} %get-tuple-element.30.shift_ref, s32[2,4]{1,0:T(2,128)} %get-tuple-element.31.sizes_ref, bf16[4,128,128]{2,1,0:T(8,128)(2,1)} %get-tuple-element.32.psi_ref, ...), custom_call_target="tpu_custom_call" | custom-call | tf_op jit(solution)/shard_map/cond/branch_0_fun/pallas_call | solution.py:341
  59.3 0.7 %shard_map.76 = (bf16[4,128,128]{2,1,0:T(8,128)(2,1)}, bf16[4,128,128]{2,1,0:T(8,128)(2,1)}, f32[5]{0:T(128)}) custom-call(bf16[4,128,128]{2,1,0:T(8,128)(2,1)S(1)} %get-tuple-element.51.kry_in, bf16[4,128,128]{2,1,0:T(8,128)(2,1)S(1)} %get-tuple-element.52.img_in, f32[1,128]{1,0:T(1,128)S(1)} %get-tuple-element.53.coef_in), custom_call_target="tpu_custom_call" | custom-call | tf_op jit(solution)/shard_map/pallas_call | solution.py:397
